TPU v7x, 32 devices: a whole 2x2x4 slice. The times are simulated.
32 devices in a mesh: groups: 2 (over x), img: 16 (over z, y, core).
Axes of the slice: x: 2, y: 2, z: 4, core: 2. Of those that a mesh axis runs over, the one named last changes fastest.
Arguments:
- features: bfloat16 [256, 64, 1024], P(('groups', 'img')), parts along dimension 0
- partners: int32 [256, 6], P('groups'), parts along dimension 0, may hold values from 0 to 127, as said below
- w_embed: bfloat16 [1024, 768], replicated, may hold values from -0.1875 to 0.1875
- b_embed: float32 [768], replicated, may hold values from -3 to 3
- gain_query: float32 [768], replicated, may hold values from 0.25 to 1.75
- gain_memory: float32 [768], replicated, may hold values from 0.25 to 1.75
- w_query: bfloat16 [768, 768], replicated
- w_key: bfloat16 [768, 768], replicated
- w_value: bfloat16 [768, 768], replicated, may hold values from -0.21875 to 0.21875
- w_out: bfloat16 [768, 768], replicated, may hold values from -0.21875 to 0.21875
- gain_head: float32 [768], replicated, may hold values from 0.25 to 1.75
- w_head: bfloat16 [7, 768], replicated, may hold values from -0.21875 to 0.21875
- b_head: float32 [7], replicated, may hold values from -3 to 3
- points: float32 [256, 3, 64], P(('groups', 'img')), parts along dimension 0, may hold values from -6 to 6
- pair_pose: float32 [12, 1536], P(None, ('groups', 'img')), parts along dimension 1, may hold values from -3 to 3
Outputs:
- new_points: float32 [256, 3, 64], P(('groups', 'img')), parts along dimension 0
- new_pose: float32 [12, 1536], P(None, ('groups', 'img')), parts along dimension 1
- loss: float32 [2], P('groups'), parts along dimension 0
There are 2 independent parts, one for each index of `groups`. A program takes and returns all parts, laid end to end along the dimension named above; an argument that names none is the same for every part. Nothing has to cross between parts.
Inputs may be any that keep to these rules, and one draw needn't show every extreme that they name: `partners`: no pair joins two images of one device. For a device s of img and any other device d, at most 4 pairs have their query image on s and their partner on d; for every s some d receives exactly 4. Images of a device are 8 consecutive numbers.
All inputs are finite; a program needn't handle non-finite values.
Results may differ from a plain program's by a relative error of at most 0.014.
Values may be sent and summed in bfloat16 or wider, within the bound.
A program may use at most 128 MiB of HBM per device.

v0:
```python
import jax
import jax.numpy as jnp
from jax import lax
from jax.sharding import PartitionSpec as P

HEADS = 12


def layer_norm(values, gain):
    center = values - jnp.mean(values, axis=-1, keepdims=True)
    spread = jnp.mean(center * center, axis=-1, keepdims=True)
    return center * lax.rsqrt(spread + 1e-06) * gain


def per_device(
    features,
    partners,
    w_embed,
    b_embed,
    gain_query,
    gain_memory,
    w_query,
    w_key,
    w_value,
    w_out,
    gain_head,
    w_head,
    b_head,
    points,
    pair_pose,
):
    maximum_value = lax.Precision.HIGHEST
    count = lax.axis_size("img")
    own_index = lax.axis_index("img")
    img_dev, tokens_img, enc_width = features.shape
    width = w_query.shape[0]
    per_img = partners.shape[1]
    views = img_dev * per_img
    heads = HEADS
    head_size = width // heads
    capacity = max(2, (views + count - 2) // (count - 1))
    slots = count * capacity
    embedded = (
        jnp.dot(features.reshape(-1, enc_width), w_embed, preferred_element_type=jnp.float32)
        + b_embed
    ).astype(jnp.bfloat16)
    embed_f = embedded.astype(jnp.float32)
    query_norm = layer_norm(embed_f, gain_query).astype(jnp.bfloat16)
    memory_norm = layer_norm(embed_f, gain_memory).astype(jnp.bfloat16)
    queries = (
        jnp.dot(query_norm, w_query, preferred_element_type=jnp.float32)
        .astype(jnp.bfloat16)
        .reshape(img_dev, tokens_img, heads, head_size)
    )
    owners = (partners // img_dev).reshape(count, views)
    local_idx = (partners % img_dev).reshape(count, views)
    view_range = jnp.arange(views)
    earlier = view_range[:, None] > view_range[None, :]
    same_owner = owners[:, :, None] == owners[:, None, :]
    rank = jnp.sum(jnp.logical_and(same_owner, earlier[None]), axis=2)
    mine = owners == own_index
    select = jnp.logical_and(
        mine[:, :, None], rank[:, :, None] == jnp.arange(capacity)[None, None, :]
    ).astype(jnp.float32)
    local_hot = (local_idx[:, :, None] == jnp.arange(img_dev)[None, None, :]).astype(jnp.float32)
    pick = jnp.einsum("svc,svl->scl", select, local_hot, precision=maximum_value)
    pick_flat = pick.reshape(slots, img_dev).astype(jnp.bfloat16)
    my_owner = lax.dynamic_index_in_dim(owners, own_index, 0, keepdims=False)
    my_rank = lax.dynamic_index_in_dim(rank, own_index, 0, keepdims=False)
    slot_of_view = my_owner * capacity + my_rank
    placed = jnp.dot(
        pick_flat,
        memory_norm.reshape(img_dev, tokens_img * width),
        preferred_element_type=jnp.float32,
    )
    arrived = lax.all_to_all(
        placed.astype(jnp.bfloat16).reshape(count, capacity, tokens_img, width),
        "img",
        split_axis=0,
        concat_axis=0,
        tiled=True,
    )
    memory_views = jnp.take(
        arrived.reshape(slots, tokens_img, width), slot_of_view, axis=0
    ).reshape(views * tokens_img, width)
    key_views = jnp.dot(memory_views, w_key, preferred_element_type=jnp.float32).astype(
        jnp.bfloat16
    )
    value_views = jnp.dot(memory_views, w_value, preferred_element_type=jnp.float32).astype(
        jnp.bfloat16
    )
    key_views = key_views.reshape(img_dev, per_img, tokens_img, heads, head_size)
    value_views = value_views.reshape(img_dev, per_img, tokens_img, heads, head_size)
    scale = 1.0 / head_size**0.5
    scores = (
        jnp.einsum("ithd,ipshd->iphts", queries, key_views, preferred_element_type=jnp.float32)
        * scale
    )
    top = jnp.max(scores, axis=-1, keepdims=True)
    expo = jnp.exp(scores - top)
    weights = (expo / jnp.sum(expo, axis=-1, keepdims=True)).astype(jnp.bfloat16)
    attended = jnp.einsum(
        "iphts,ipshd->ipthd", weights, value_views, preferred_element_type=jnp.float32
    ).astype(jnp.bfloat16)
    projected = jnp.dot(
        attended.reshape(views * tokens_img, width), w_out, preferred_element_type=jnp.float32
    )
    decoded = embed_f.reshape(img_dev, 1, tokens_img, width) + projected.reshape(
        img_dev, per_img, tokens_img, width
    )
    head_in = layer_norm(decoded, gain_head).astype(jnp.bfloat16)
    pred = (
        jnp.einsum("iptd,cd->ipct", head_in, w_head, preferred_element_type=jnp.float32)
        + b_head[None, None, :, None]
    )
    pred = pred.reshape(views, 7, tokens_img)
    second_view_point = pred[:, 0:3]
    first_view_point = pred[:, 3:6]
    certainty_level = 1.0 + jnp.exp(pred[:, 6])
    pose_rows = pair_pose.T
    linear_transform = pose_rows[:, 0:9].reshape(views, 3, 3)
    translation_vector = pose_rows[:, 9:12]
    second_world_point = (
        jnp.einsum("xdp,xpk->xdk", linear_transform, second_view_point, precision=maximum_value)
        + translation_vector[:, :, None]
    )
    first_world_point = (
        jnp.einsum("xdp,xpk->xdk", linear_transform, first_view_point, precision=maximum_value)
        + translation_vector[:, :, None]
    )
    chi_views = jnp.broadcast_to(points[:, None], (img_dev, per_img, 3, tokens_img)).reshape(
        views, 3, tokens_img
    )
    second_residual = chi_views - second_world_point
    weighted_q = (certainty_level[:, None] * second_residual).reshape(
        img_dev, per_img, 3, tokens_img
    )
    grad_q = jnp.sum(weighted_q, axis=1)
    total_q = jnp.sum(certainty_level.reshape(img_dev, per_img, tokens_img), axis=1)
    gradient_transform = -2.0 * jnp.einsum(
        "zo,zpo,zso->zps",
        certainty_level,
        second_residual,
        second_view_point,
        precision=maximum_value,
    )
    grad_off = -2.0 * jnp.sum(certainty_level[:, None] * second_residual, axis=2)
    denom = 4.0 * jnp.sum(certainty_level, axis=1)
    grads = jnp.concatenate([gradient_transform.reshape(views, 9), grad_off], axis=1)
    new_pose = (pose_rows - grads / denom[:, None]).T
    err_q = jnp.sum(certainty_level * jnp.sum(second_residual * second_residual, axis=1))
    payload = jnp.concatenate([first_world_point, certainty_level[:, None]], axis=1)
    slot_hot = (slot_of_view[:, None] == jnp.arange(slots)[None, :]).astype(jnp.float32)
    outgoing = jnp.einsum("vk,vct->kct", slot_hot, payload, precision=maximum_value).reshape(
        count, capacity, 4, tokens_img
    )
    returned = lax.all_to_all(
        outgoing.astype(jnp.bfloat16), "img", split_axis=0, concat_axis=0, tiled=True
    ).astype(outgoing.dtype)
    ret_world = returned[:, :, 0:3]
    ret_conf = returned[:, :, 3]
    chi_slot = jnp.einsum("scl,lat->scat", pick, points, precision=maximum_value)
    res_p = chi_slot - ret_world
    grad_p = jnp.einsum(
        "scl,scat->lat", pick, ret_conf[:, :, None] * res_p, precision=maximum_value
    )
    total_p = jnp.einsum("scl,sct->lt", pick, ret_conf, precision=maximum_value)
    err_p = jnp.sum(ret_conf * jnp.sum(res_p * res_p, axis=2))
    new_points = points - 0.5 * (grad_q + grad_p) / (total_q + total_p)[:, None, :]
    err_sum, weight_sum = lax.psum((err_q + err_p, 2.0 * jnp.sum(certainty_level)), "img")
    loss = (err_sum / weight_sum).reshape(1)
    return (new_points, new_pose, loss)


def solution(mesh):
    return jax.shard_map(
        per_device,
        mesh=mesh,
        in_specs=(
            P(("groups", "img"), None, None),
            P("groups", None),
            P(),
            P(),
            P(),
            P(),
            P(),
            P(),
            P(),
            P(),
            P(),
            P(),
            P(),
            P(("groups", "img"), None, None),
            P(None, ("groups", "img")),
        ),
        out_specs=(P(("groups", "img"), None, None), P(None, ("groups", "img")), P("groups")),
        check_vma=False,
    )
```

profile of v0, /device:TPU:0, one launch (start us, length us, event | category | flops | bytes accessed | tf_op | source)
XLA Modules:
  0.0 324.6 jit_solution(6641877733318594843)
XLA Ops:
  0.6 0.0 copy-start
  0.7 1.4 copy-done
  2.0 2.3 fusion.64
  4.4 0.3 multiply_reduce_fusion.1
  4.7 0.3 multiply_convert_fusion.3
  5.0 0.4 reshape.178
  5.4 0.1 copy.97
  5.5 0.1 reshape.177
  5.6 0.5 convert_reduce_fusion
  6.0 0.1 copy.98
  6.2 0.1 eq.74
  6.2 0.2 fusion.63
  6.4 1.8 convolution_convert_fusion
  8.2 4.3 %copy.138 = bf16[8,8,64,768]{3,2,1,0:T(8,128)(2,1)} copy(bf16[8,8,64,768]{3,1,2,0:T(8,128)(2,1)S(1)} %bitcast.122) | data formatting | bytes 12582912
  12.5 7.6 %all-to-all-start = ((bf16[16,4,64,768]{3,2,1,0:T(8,128)(2,1)}), bf16[16,4,64,768]{3,2,1,0:T(8,128)(2,1)}, u32[]{:S(2)}, u32[]{:S(2)}) async-start(bf16[16,4,64,768]{3,2,1,0:T(8,128)(2,1)} %bitcast.121), calls=%async_computation | async-start | bytes 12582912 | tf_op jit(solution)/shard_map/all_to_all | solution.py:76
  20.0 0.0 copy-start.5
  20.0 0.0 copy-start.4
  20.1 0.1 broadcast_in_dim.13
  20.2 0.1 broadcast_in_dim.14
  20.3 2.1 convolution_convert_fusion.3
  22.4 2.2 reshape.207
  24.6 0.1 copy.106
  24.8 0.1 copy.107
  24.9 0.1 copy.113
  25.0 109.3 %all-to-all-done = bf16[16,4,64,768]{3,2,1,0:T(8,128)(2,1)} async-done(((bf16[16,4,64,768]{3,2,1,0:T(8,128)(2,1)}), bf16[16,4,64,768]{3,2,1,0:T(8,128)(2,1)}, u32[]{:S(2)}, u32[]{:S(2)}) %all-to-all-start) | async-done | bytes 6291488 | tf_op jit(solution)/shard_map/all_to_all | solution.py:76
  134.2 6.0 %gather_fusion = bf16[48,64,768]{2,1,0:T(8,128)(2,1)} fusion(bf16[64,64,768]{2,1,0:T(8,128)(2,1)} %bitcast.4, s32[1024]{0:T(1024)S(1)} %pad_clamp_fusion), kind=kCustom, calls=%fused_computation | custom fusion | bytes 9437376 | tf_op jit(solution)/shard_map/jit(_take)/gather | solution.py:83
  140.2 3.4 %bitcast_select_fusion = bf16[3072,768]{1,0:T(8,128)(2,1)S(1)} fusion(bf16[48,64,768]{2,1,0:T(8,128)(2,1)} %gather_fusion, pred[3072]{0:T(1024)(128)(4,1)S(1)} %broadcast_in_dim.14), kind=kLoop, calls=%fused_computation.21 | loop fusion | flops 2359296 | bytes 9440256 | tf_op jit(solution)/shard_map/jit(_take)/select_n | solution.py:83
  143.6 0.0 copy-start.2
  143.6 2.1 copy-done.2
  145.8 5.5 %convolution_convert_fusion.1 = bf16[3072,768]{1,0:T(8,128)(2,1)} fusion(bf16[3072,768]{1,0:T(8,128)(2,1)S(1)} %bitcast_select_fusion, bf16[768,768]{1,0:T(8,128)(2,1)S(1)} %copy-done.11), kind=kOutput, calls=%fused_computation.19 | convolution fusion | flops 3626237952 | bytes 10616832 | tf_op jit(solution)/shard_map/dot_general | solution.py:86
  151.2 14.9 %reshape.182 = bf16[8,6,64,12,64]{4,3,2,1,0:T(8,128)(2,1)} reshape(bf16[3072,768]{1,0:T(8,128)(2,1)} %convolution_convert_fusion.1) | data formatting | bytes 9437184 | tf_op jit(solution)/shard_map/reshape | solution.py:92
  166.2 11.9 %fusion.9 = f32[8,12,6,64,64]{4,3,2,1,0:T(8,128)} fusion(bf16[8,6,64,12,64]{4,3,2,1,0:T(8,128)(2,1)} %reshape.182, bf16[8,64,12,64,1]{3,2,1,0,4:T(8,128)(2,1)} %bitcast.123), kind=kOutput, calls=%fused_computation.12 | convolution fusion | flops 301989888 | bytes 14942208 | tf_op jit(solution)/shard_map/ithd,ipshd->iphts/dot_general | solution.py:96
  178.1 21.4 %fusion.65 = (f32[8,6,12,64]{3,1,2,0:T(8,128)S(1)}, f32[8,6,12,64,64]{3,4,1,2,0:T(8,128)}) fusion(f32[8,12,6,64,64]{4,3,2,1,0:T(8,128)} %fusion.9), kind=kOutput, calls=%fused_computation.113 | output fusion | flops 9437247 | bytes 19021824 | tf_op jit(solution)/shard_map/sub | solution.py:100
  199.4 7.8 %convolution_convert_fusion.2 = bf16[3072,768]{1,0:T(8,128)(2,1)} fusion(bf16[3072,768]{1,0:T(8,128)(2,1)} %copy-done.2, bf16[768,768]{1,0:T(8,128)(2,1)S(1)} %copy-done.12), kind=kOutput, calls=%fused_computation.20 | convolution fusion | flops 3626237952 | bytes 10616832 | tf_op jit(solution)/shard_map/dot_general | solution.py:89
  207.3 15.0 %reshape.181 = bf16[8,6,64,12,64]{4,3,2,1,0:T(8,128)(2,1)} reshape(bf16[3072,768]{1,0:T(8,128)(2,1)} %convolution_convert_fusion.2) | data formatting | bytes 9437184 | tf_op jit(solution)/shard_map/reshape | solution.py:93
  222.2 15.6 %fusion.12 = bf16[8,6,12,64,64]{4,3,2,1,0:T(8,128)(2,1)} fusion(bf16[8,6,64,12,64]{4,3,2,1,0:T(8,128)(2,1)} %reshape.181, f32[8,6,12,64,64]{3,4,1,2,0:T(8,128)} %get-tuple-element.21, f32[8,6,12,64]{3,1,2,0:T(8,128)S(1)} %get-tuple-element.20), kind=kOutput, calls=%fused_computation.18 | convolution fusion | flops 309067776 | bytes 19021824 | tf_op jit(solution)/shard_map/iphts,ipshd->ipthd/dot_general | solution.py:102
  237.9 7.3 %add_reduce_fusion = (f32[8,6,64]{2,1,0:T(8,128)S(1)}, f32[8,6,64,768]{3,2,1,0:T(8,128)S(1)}) fusion(f32[8,64,768]{2,1,0:T(8,128)S(1)} %bitcast.118, bf16[8,6,64,768]{2,3,1,0:T(8,128)(2,1)} %bitcast.124, bf16[768,768]{1,0:T(8,128)(2,1)S(1)} %copy-done.3), kind=kOutput, calls=%fused_computation.17 | convolution fusion | flops 3628594176 | bytes 16920576 | tf_op jit(solution)/shard_map/dot_general | solution.py:105
  245.2 0.0 copy-start.6
  245.2 0.0 copy-start.8
  245.2 0.0 copy-start.10
  245.2 1.7 multiply_reduce_fusion
  247.0 0.0 copy-start.1
  247.0 2.3 fusion.22
  249.3 0.5 broadcast.156
  249.9 1.5 fusion.60
  251.4 0.5 fusion.23
  251.8 0.1 pad_maximum_fusion
  251.9 0.3 convolution_convert_fusion.4
  252.2 0.1 copy.110
  252.3 0.7 reshape.217
  253.0 28.1 %all-to-all-start.1 = ((bf16[16,2,512]{2,1,0:T(2,128)(2,1)}), bf16[16,2,512]{2,1,0:T(2,128)(2,1)S(1)}, u32[]{:S(2)}, u32[]{:S(2)}) async-start(bf16[16,2,512]{2,1,0:T(2,128)(2,1)} %reshape.217), calls=%async_computation.1 | async-start | bytes 65536 | tf_op jit(solution)/shard_map/all_to_all | solution.py:157
  281.1 0.6 fusion.61
  281.7 0.4 convolution_multiply_fusion
  282.1 0.1 copy.118
  282.2 0.1 copy.119
  283.1 0.6 fusion.55
  283.7 0.6 multiply_reduce_fusion.5
  284.3 3.4 %all-to-all-done.1 = bf16[16,2,512]{2,1,0:T(2,128)(2,1)S(1)} async-done(((bf16[16,2,512]{2,1,0:T(2,128)(2,1)}), bf16[16,2,512]{2,1,0:T(2,128)(2,1)S(1)}, u32[]{:S(2)}, u32[]{:S(2)}) %all-to-all-start.1) | async-done | bytes 32800 | tf_op jit(solution)/shard_map/all_to_all | solution.py:157
  287.7 0.1 reshape.218
  287.9 0.2 multiply_reduce_fusion.2
  288.1 0.6 multiply_reduce_fusion.4
  290.0 30.9 %all-reduce = (f32[]{:T(128)}, f32[]{:T(128)}) all-reduce(f32[]{:T(128)S(6)} %add.182, f32[]{:T(128)S(6)} %mul_shard_map.3), channel_id=1, replica_groups=mesh['groups'=2,'img'=16] {'img'}, use_global_device_ids=true, to_apply=%region_15.16 | all-reduce | flops 2 | bytes 16 | tf_op jit(solution)/shard_map/psum | solution.py:170
  322.3 0.2 fusion.30
  322.5 0.9 fusion.29
  (41 shorter events, 0.3 us)
Async XLA Ops:
  0.6 1.4 copy-start
  2.0 2.6 copy-start.7
  4.3 1.0 copy-start.9
  12.5 7.8 %copy-start.13 = (f32[768]{0:T(1024)S(1)}, f32[768]{0:T(1024)}, u32[]{:S(2)}) copy-start(f32[768]{0:T(1024)} %param.19) | copy-start | bytes 9220
  12.5 121.8 %all-to-all-start = ((bf16[16,4,64,768]{3,2,1,0:T(8,128)(2,1)}), bf16[16,4,64,768]{3,2,1,0:T(8,128)(2,1)}, u32[]{:S(2)}, u32[]{:S(2)}) async-start(bf16[16,4,64,768]{3,2,1,0:T(8,128)(2,1)} %bitcast.121), calls=%async_computation | async-start | bytes 12582912 | tf_op jit(solution)/shard_map/all_to_all | solution.py:76
  20.0 4.6 %copy-start.5 = (f32[12,48]{1,0:T(8,128)S(1)}, f32[12,48]{1,0:T(8,128)}, u32[]{:S(2)}) copy-start(f32[12,48]{1,0:T(8,128)} %param.29) | copy-start | bytes 6916
  20.0 4.8 %copy-start.4 = (f32[8,3,64]{2,0,1:T(8,128)S(1)}, f32[8,3,64]{2,0,1:T(8,128)}, u32[]{:S(2)}) copy-start(f32[8,3,64]{2,0,1:T(8,128)} %param.28) | copy-start | bytes 18436
  140.2 5.5 %copy-start.11 = (bf16[768,768]{1,0:T(8,128)(2,1)S(1)}, bf16[768,768]{1,0:T(8,128)(2,1)}, u32[]{:S(2)}) copy-start(bf16[768,768]{1,0:T(8,128)(2,1)} %param.22) | copy-start | bytes 3538948
  143.6 2.2 copy-start.2
  178.1 21.4 %copy-start.12 = (bf16[768,768]{1,0:T(8,128)(2,1)S(1)}, bf16[768,768]{1,0:T(8,128)(2,1)}, u32[]{:S(2)}) copy-start(bf16[768,768]{1,0:T(8,128)(2,1)} %param.23) | copy-start | bytes 3538948
  222.2 15.6 %copy-start.3 = (bf16[768,768]{1,0:T(8,128)(2,1)S(1)}, bf16[768,768]{1,0:T(8,128)(2,1)}, u32[]{:S(2)}) copy-start(bf16[768,768]{1,0:T(8,128)(2,1)} %param.24) | copy-start | bytes 3538948
  245.2 1.8 copy-start.6
  245.2 1.8 copy-start.8
  245.2 1.8 copy-start.10
  247.0 76.5 %copy-start.1 = (bf16[1024,768]{1,0:T(8,128)(2,1)S(1)}, bf16[1024,768]{1,0:T(8,128)(2,1)}, u32[]{:S(2)}) copy-start(bf16[1024,768]{1,0:T(8,128)(2,1)} %param.17) | copy-start | bytes 4718596
  253.0 34.7 %all-to-all-start.1 = ((bf16[16,2,512]{2,1,0:T(2,128)(2,1)}), bf16[16,2,512]{2,1,0:T(2,128)(2,1)S(1)}, u32[]{:S(2)}, u32[]{:S(2)}) async-start(bf16[16,2,512]{2,1,0:T(2,128)(2,1)} %reshape.217), calls=%async_computation.1 | async-start | bytes 65536 | tf_op jit(solution)/shard_map/all_to_all | solution.py:157
where the time goes:
time: 326 us; the launch traced here: 325 us
  waiting for transfers between devices  113 us (35%)
  matrix products  59.9 us (18%)
  local copies, waits for them, and re-layouts  48.9 us (15%)
  starting transfers between devices  35.6 us (11%)
  other arithmetic  31.1 us (10%)
  blocking collectives  30.9 us (9%)
  between operations  5.43 us (2%)
    all_to_all x1, waiting for transfers between devices, per_device(): lax.all_to_all(placed.astype(jnp.bfloat16).reshape(count, capacity, token...  109 us
    psum x1, blocking collectives, per_device(): lax.psum((err_q + err_p, 2.0 * jnp.sum(certainty_level)), 'img')  30.9 us
    all_to_all x1, starting transfers between devices, per_device(): lax.all_to_all(outgoing.astype(jnp.bfloat16), 'img', split_axis=0, concat...  28.1 us
    sub x1, other arithmetic, per_device(): expo = jnp.exp(scores - top)  21.4 us
    dot_general x1, matrix products, per_device(): jnp.einsum('iphts,ipshd->ipthd', weights, value_views, preferred_element_...  15.6 us
    reshape x1, local copies, waits for them, and re-layouts, per_device(): value_views.reshape(img_dev, per_img, tokens_img, heads, head_size)  15 us
    reshape x1, local copies, waits for them, and re-layouts, per_device(): key_views.reshape(img_dev, per_img, tokens_img, heads, head_size)  14.9 us
    dot_general x1, matrix products, per_device(): jnp.einsum('ithd,ipshd->iphts', queries, key_views, preferred_element_typ...  11.9 us
  transfers between devices with their start and end apart: 2, of which 2 were waited for; matrix products, arithmetic and copies ran while one was open for 2% of the time, Pallas kernels for 0%

commit v1 on v0

--- a/solution.py
+++ b/solution.py
@@ -1,9 +1,508 @@
+import functools
+
 import jax
 import jax.numpy as jnp
 from jax import lax
+from jax.experimental import pallas as pl
+from jax.experimental.pallas import tpu as pltpu
 from jax.sharding import PartitionSpec as P
 
 HEADS = 12
+IMGS = 8
+PER = 6
+TOK = 64
+VIEWS = IMGS * PER
+E = 1024
+D = 768
+NDEV = 16
+ALL = NDEV * IMGS
+CHUNKS = 2
+CROWS = IMGS * TOK // CHUNKS
+CIMG = IMGS // CHUNKS
+UP, DOWN, ACROSS, SIB = 0, 1, 2, 3
+F32, BF16 = jnp.float32, jnp.bfloat16
+HI = lax.Precision.HIGHEST
+
+
+def norm_rows(values, gain):
+    center = values - jnp.mean(values, axis=-1, keepdims=True)
+    spread = jnp.mean(center * center, axis=-1, keepdims=True)
+    return center * lax.rsqrt(spread + 1e-06) * gain
+
+
+def dot(a, b, dims=((1,), (0,)), precision=None):
+    return lax.dot_general(a, b, (dims, ((), ())), precision=precision, preferred_element_type=F32)
+
+
+def kernel(
+    features,
+    partners_s,
+    partners_v,
+    w_embed,
+    b_embed,
+    gain_query,
+    gain_memory,
+    w_query,
+    w_key,
+    w_value,
+    w_out,
+    gain_head,
+    w_head,
+    b_head,
+    points,
+    pair_pose,
+    new_points,
+    new_pose,
+    loss,
+    feat,
+    we,
+    wq,
+    wk,
+    wv,
+    wo,
+    memory,
+    keys,
+    values,
+    embedded,
+    query_norm,
+    query_diag,
+    attended,
+    pred,
+    all_points,
+    outgoing,
+    incoming,
+    load_sem,
+    send_sem,
+    recv_sem,
+    pts_send,
+    pts_recv,
+    out_send,
+    out_recv,
+):
+    own = lax.axis_index("img")
+    core = own % 2
+    y = (own // 2) % 2
+    z = own // 4
+
+    barrier = pltpu.get_barrier_semaphore()
+    for k in range(1, NDEV):
+        pl.semaphore_signal(
+            barrier,
+            inc=1,
+            device_id={"img": (own + k) % NDEV},
+            device_id_type=pl.DeviceIdType.MESH,
+        )
+
+    loads = []
+    for slot, (src, dst) in enumerate(
+        [(features, feat), (w_embed, we), (w_query, wq), (w_key, wk), (w_value, wv), (w_out, wo)]
+    ):
+        copy = pltpu.make_async_copy(src, dst, load_sem.at[slot])
+        copy.start()
+        loads.append(copy)
+
+    def rank_of(zz, yy, cc):
+        return (zz * 2 + yy) * 2 + cc
+
+    targets = {
+        UP: own + 4,
+        DOWN: own - 4,
+        ACROSS: rank_of(z, 1 - y, core),
+        SIB: rank_of(z, y, 1 - core),
+    }
+
+    def move(piece, way):
+        return pltpu.make_async_remote_copy(
+            src_ref=memory.at[piece],
+            dst_ref=memory.at[piece],
+            send_sem=send_sem.at[piece * 4 + way],
+            recv_sem=recv_sem.at[piece],
+            device_id={"img": targets[way]},
+            device_id_type=pl.DeviceIdType.MESH,
+        )
+
+    def arrive(piece):
+        move(piece, SIB).wait_recv()
+
+    side = z // 2
+    near = z * (1 - side) + (3 - z) * side
+
+    def origin_z(j):
+        first = (4 - j) // 3 - (3 - j) // 3
+        f = (j - near * first) * (1 - side) + (3 - j + near * first) * side
+        zero = (3 - j) // 3
+        return zero * z + (1 - zero) * f
+
+    def forward_z(oz, piece):
+        @pl.when((oz < z) & (z < 3))
+        def _():
+            move(piece, UP).start()
+
+        @pl.when((oz > z) & (z > 0))
+        def _():
+            move(piece, DOWN).start()
+
+    def points_copy(peer, slot):
+        return pltpu.make_async_remote_copy(
+            src_ref=all_points.at[own],
+            dst_ref=all_points.at[own],
+            send_sem=pts_send.at[slot],
+            recv_sem=pts_recv.at[own],
+            device_id={"img": peer},
+            device_id_type=pl.DeviceIdType.MESH,
+        )
+
+    def points_arrive(peer, slot):
+        pltpu.make_async_remote_copy(
+            src_ref=all_points.at[peer],
+            dst_ref=all_points.at[peer],
+            send_sem=pts_send.at[slot],
+            recv_sem=pts_recv.at[peer],
+            device_id={"img": peer},
+            device_id_type=pl.DeviceIdType.MESH,
+        ).wait_recv()
+
+    all_points[own] = jnp.concatenate(
+        [points[:, 0, :], points[:, 1, :], points[:, 2, :], points[:, 2, :]], axis=1
+    )
+
+    loads[0].wait()
+    loads[1].wait()
+    for ch in range(CHUNKS):
+        rows = pl.ds(ch * CROWS, CROWS)
+        emb = (dot(feat[rows, :], we[...]) + b_embed[...]).astype(BF16)
+        embedded[rows, :] = emb
+        emb_f = emb.astype(F32)
+        center = emb_f - jnp.mean(emb_f, axis=-1, keepdims=True)
+        unit = center * lax.rsqrt(jnp.mean(center * center, axis=-1, keepdims=True) + 1e-06)
+        memory[own * CHUNKS + ch] = (unit * gain_memory[...]).astype(BF16)
+        query_norm[rows, :] = (unit * gain_query[...]).astype(BF16)
+        if ch == 0:
+            pl.semaphore_wait(barrier, NDEV - 1)
+            for k in range(1, NDEV):
+                points_copy((own + k) % NDEV, k).start()
+        piece = own * CHUNKS + ch
+
+        move(piece, ACROSS).start()
+
+        @pl.when(z < 3)
+        def _():
+            move(piece, UP).start()
+
+        @pl.when(z > 0)
+        def _():
+            move(piece, DOWN).start()
+
+        move(piece, SIB).start()
+
+    loads[2].wait()
+    group = lax.broadcasted_iota(jnp.int32, (256, 256), 0) // 64
+    same_head = group == lax.broadcasted_iota(jnp.int32, (256, 256), 1) // 64
+
+    def make_queries(i, carry):
+        rows = pl.ds(pl.multiple_of(i * TOK, TOK), TOK)
+        q = dot(query_norm[rows, :], wq[...]).astype(BF16).astype(F32) * 0.125
+        for g in range(3):
+            part = q[:, g * 256 : (g + 1) * 256]
+            stacked = jnp.concatenate([part] * 4, axis=0)
+            query_diag[i * 3 + g] = jnp.where(same_head, stacked, 0.0).astype(BF16)
+        return carry
+
+    lax.fori_loop(0, IMGS, make_queries, 0)
+
+    loads[3].wait()
+    loads[4].wait()
+    loads[5].wait()
+
+    def project(piece):
+        rows = memory[piece]
+        at = pl.ds(piece * CIMG, CIMG)
+        keys[at] = dot(rows, wk[...]).astype(BF16).reshape(CIMG, TOK, D)
+        values[at] = dot(rows, wv[...]).astype(BF16).reshape(CIMG, TOK, D)
+
+    def exchange(step, carry):
+        j = 1 + step // CHUNKS
+        ch = step % CHUNKS
+        oz = origin_z(j)
+        oy = origin_z(j - 1)
+        from_z = rank_of(oz, y, core) * CHUNKS + ch
+        from_y = rank_of(oy, 1 - y, core) * CHUNKS + ch
+        arrive(from_z)
+        forward_z(oz, from_z)
+        move(from_z, ACROSS).start()
+        move(from_z, SIB).start()
+        project(from_z)
+        arrive(from_y)
+        move(from_y, SIB).start()
+        project(from_y)
+        sib_z = rank_of(oy, y, 1 - core) * CHUNKS + ch
+        arrive(sib_z)
+        project(sib_z)
+        return carry
+
+    lax.fori_loop(0, 3 * CHUNKS, exchange, 0)
+
+    def finish(ch, carry):
+        oz = origin_z(3)
+        from_y = rank_of(oz, 1 - y, core) * CHUNKS + ch
+        arrive(from_y)
+        move(from_y, SIB).start()
+        sib_z = rank_of(oz, y, 1 - core) * CHUNKS + ch
+        arrive(sib_z)
+        project(sib_z)
+        project(from_y)
+        return carry
+
+    def sibling_rest(step, carry):
+        sib_y = rank_of(origin_z(step // CHUNKS), 1 - y, 1 - core) * CHUNKS + step % CHUNKS
+        arrive(sib_y)
+        project(sib_y)
+        return carry
+
+    lax.fori_loop(0, 3 * CHUNKS, sibling_rest, 0)
+    lax.fori_loop(0, CHUNKS, finish, 0)
+    lax.fori_loop(3 * CHUNKS, 4 * CHUNKS, sibling_rest, 0)
+
+    for k in range(1, NDEV):
+        points_arrive((own + k) % NDEV, k)
+        points_copy((own + k) % NDEV, k).wait_send()
+
+    lane = lax.broadcasted_iota(jnp.int32, (TOK, 128), 1)
+
+    def image(i, carry):
+        ids = [partners_s[own * VIEWS + i * PER + p] for p in range(PER)]
+        key_rows = jnp.concatenate([keys[ids[p]] for p in range(PER)], axis=0)
+        for g in range(3):
+            scores = dot(
+                key_rows[:, g * 256 : (g + 1) * 256], query_diag[i * 3 + g], ((1,), (1,))
+            ).reshape(PER, TOK, 256)
+            expo = jnp.exp(scores - jnp.max(scores, axis=1, keepdims=True))
+            weights = (expo * (1.0 / jnp.sum(expo, axis=1, keepdims=True))).astype(BF16)
+            for p in range(PER):
+                for half in range(2):
+                    lo = g * 256 + half * 128
+                    both = dot(
+                        weights[p, :, half * 128 : half * 128 + 128],
+                        values[ids[p], :, lo : lo + 128],
+                        ((0,), (0,)),
+                    )
+                    attended[p * TOK : (p + 1) * TOK, lo : lo + 128] = jnp.where(
+                        lane < 64, both[:64], both[64:]
+                    ).astype(BF16)
+        projected = dot(attended[...], wo[...])
+        emb_f = embedded[pl.ds(pl.multiple_of(i * TOK, TOK), TOK), :].astype(F32)
+        decoded = projected.reshape(PER, TOK, D) + emb_f[None]
+        head_in = norm_rows(decoded, gain_head[...].reshape(1, 1, D)).astype(BF16)
+        out = dot(w_head[...], head_in.reshape(PER * TOK, D), ((1,), (1,)))
+        for p in range(PER):
+            pred[p * IMGS + i, 0:7, :] = out[:, p * TOK : (p + 1) * TOK]
+        return carry
+
+    lax.fori_loop(0, IMGS, image, 0)
+
+    x = [pred[:, c, :] + b_head[c] for c in range(7)]
+    conf = 1.0 + jnp.exp(x[6])
+    mine = partners_v[pl.ds(pl.multiple_of(own * IMGS, IMGS), IMGS), :]
+    ids = jnp.concatenate([mine[:, p : p + 1] for p in range(PER)], axis=0)
+    hot = (ids == lax.broadcasted_iota(jnp.int32, (VIEWS, ALL), 1)).astype(F32)
+    row = lax.broadcasted_iota(jnp.int32, (VIEWS, VIEWS), 0)
+    col = lax.broadcasted_iota(jnp.int32, (VIEWS, VIEWS), 1)
+    perm = ((row % IMGS) * PER + row // IMGS == col).astype(F32)
+    pose = dot(perm, pair_pose[...], ((1,), (1,)), HI)
+    partner_pts = dot(hot, all_points[...].reshape(ALL, 256), precision=HI)
+    res_q, res_p = [], []
+    for a in range(3):
+        m = [pose[:, 3 * a + b : 3 * a + b + 1] for b in range(3)]
+        off = pose[:, 9 + a : 10 + a]
+        world_q = m[0] * x[0] + m[1] * x[1] + m[2] * x[2] + off
+        world_p = m[0] * x[3] + m[1] * x[4] + m[2] * x[5] + off
+        chi = jnp.concatenate([points[:, a, :]] * PER, axis=0)
+        res_q.append(chi - world_q)
+        res_p.append(partner_pts[:, a * TOK : (a + 1) * TOK] - world_p)
+    cq = [conf * r for r in res_q]
+    grad_rows = [
+        jnp.sum(cq[a] * x[b], axis=1, keepdims=True) for a in range(3) for b in range(3)
+    ] + [jnp.sum(cq[a], axis=1, keepdims=True) for a in range(3)]
+    conf_row = jnp.sum(conf, axis=1, keepdims=True)
+    step = jnp.concatenate(grad_rows, axis=1) * (2.0 / (4.0 * conf_row))
+    new_pose[...] = pair_pose[...] + dot(step, perm, ((0,), (0,)), HI)
+    err = jnp.sum(
+        conf
+        * (
+            res_q[0] * res_q[0]
+            + res_q[1] * res_q[1]
+            + res_q[2] * res_q[2]
+            + res_p[0] * res_p[0]
+            + res_p[1] * res_p[1]
+            + res_p[2] * res_p[2]
+        )
+    )
+    conf_sum = 2.0 * jnp.sum(conf_row)
+    payload = jnp.concatenate([conf * res_p[0], conf * res_p[1], conf * res_p[2], conf], axis=1)
+    sums = dot(hot, payload, ((0,), (0,)), HI)
+    outgoing[:, :, 0:256] = sums.reshape(NDEV, IMGS, 256)
+    tail_lane = lax.broadcasted_iota(jnp.int32, (NDEV, IMGS, 128), 2)
+    outgoing[:, :, 256:384] = jnp.where(tail_lane < 64, err, conf_sum)
+
+    def out_copy(peer, slot):
+        return pltpu.make_async_remote_copy(
+            src_ref=outgoing.at[peer],
+            dst_ref=incoming.at[own],
+            send_sem=out_send.at[slot],
+            recv_sem=out_recv.at[own],
+            device_id={"img": peer},
+            device_id_type=pl.DeviceIdType.MESH,
+        )
+
+    for k in range(1, NDEV):
+        out_copy((own + k) % NDEV, k).start()
+    incoming[own] = outgoing[own]
+
+    def fold(values):
+        total = values[0:IMGS]
+        for p in range(1, PER):
+            total = total + values[p * IMGS : (p + 1) * IMGS]
+        return total
+
+    total_q = fold(conf)
+    grad_q = [fold(c) for c in cq]
+
+    def drain(t, carry):
+        j = t // CHUNKS
+        ch = t % CHUNKS
+        oz = origin_z(j)
+        from_z = rank_of(oz, y, core) * CHUNKS + ch
+        move(from_z, ACROSS).wait_send()
+        move(from_z, SIB).wait_send()
+        move(rank_of(oz, 1 - y, core) * CHUNKS + ch, SIB).wait_send()
+
+        @pl.when((oz <= z) & (z < 3))
+        def _():
+            move(from_z, UP).wait_send()
+
+        @pl.when((oz >= z) & (z > 0))
+        def _():
+            move(from_z, DOWN).wait_send()
+
+        return carry
+
+    lax.fori_loop(0, 4 * CHUNKS, drain, 0)
+
+    for k in range(1, NDEV):
+        peer = (own + k) % NDEV
+        pltpu.make_async_remote_copy(
+            src_ref=outgoing.at[peer],
+            dst_ref=incoming.at[peer],
+            send_sem=out_send.at[k],
+            recv_sem=out_recv.at[peer],
+            device_id={"img": peer},
+            device_id_type=pl.DeviceIdType.MESH,
+        ).wait_recv()
+        out_copy(peer, k).wait_send()
+    received = jnp.sum(incoming[...], axis=0)
+    total = total_q + received[:, 192:256]
+    for a in range(3):
+        grad = grad_q[a] + received[:, a * TOK : (a + 1) * TOK]
+        new_points[:, a, :] = points[:, a, :] - 0.5 * grad / total
+    loss[...] = received[0:1, 256:257] / received[0:1, 320:321]
+
+
+def fused(*args):
+    (
+        features,
+        partners,
+        w_embed,
+        b_embed,
+        gain_query,
+        gain_memory,
+        w_query,
+        w_key,
+        w_value,
+        w_out,
+        gain_head,
+        w_head,
+        b_head,
+        points,
+        pair_pose,
+    ) = args
+    hbm = pl.BlockSpec(memory_space=pl.ANY)
+    vmem = pl.BlockSpec(memory_space=pltpu.VMEM)
+    smem = pl.BlockSpec(memory_space=pltpu.SMEM)
+    rows = IMGS * TOK
+    new_points, new_pose, loss = pl.pallas_call(
+        kernel,
+        out_shape=(
+            jax.ShapeDtypeStruct((IMGS, 3, TOK), F32),
+            jax.ShapeDtypeStruct((12, VIEWS), F32),
+            jax.ShapeDtypeStruct((1, 1), F32),
+        ),
+        in_specs=[
+            hbm,
+            smem,
+            vmem,
+            hbm,
+            vmem,
+            vmem,
+            vmem,
+            hbm,
+            hbm,
+            hbm,
+            hbm,
+            vmem,
+            vmem,
+            smem,
+            vmem,
+            vmem,
+        ],
+        out_specs=(vmem, vmem, vmem),
+        scratch_shapes=[
+            pltpu.VMEM((rows, E), BF16),
+            pltpu.VMEM((E, D), BF16),
+            pltpu.VMEM((D, D), BF16),
+            pltpu.VMEM((D, D), BF16),
+            pltpu.VMEM((D, D), BF16),
+            pltpu.VMEM((D, D), BF16),
+            pltpu.VMEM((NDEV * CHUNKS, CROWS, D), BF16),
+            pltpu.VMEM((ALL, TOK, D), BF16),
+            pltpu.VMEM((ALL, TOK, D), BF16),
+            pltpu.VMEM((rows, D), BF16),
+            pltpu.VMEM((rows, D), BF16),
+            pltpu.VMEM((IMGS * 3, 256, 256), BF16),
+            pltpu.VMEM((PER * TOK, D), BF16),
+            pltpu.VMEM((VIEWS, 8, TOK), F32),
+            pltpu.VMEM((NDEV, IMGS, 256), F32),
+            pltpu.VMEM((NDEV, IMGS, 384), F32),
+            pltpu.VMEM((NDEV, IMGS, 384), F32),
+            pltpu.SemaphoreType.DMA((6,)),
+            pltpu.SemaphoreType.DMA((NDEV * CHUNKS * 4,)),
+            pltpu.SemaphoreType.DMA((NDEV * CHUNKS,)),
+            pltpu.SemaphoreType.DMA((NDEV,)),
+            pltpu.SemaphoreType.DMA((NDEV,)),
+            pltpu.SemaphoreType.DMA((NDEV,)),
+            pltpu.SemaphoreType.DMA((NDEV,)),
+        ],
+        compiler_params=pltpu.CompilerParams(
+            collective_id=0, has_side_effects=True, vmem_limit_bytes=62 * 1024 * 1024
+        ),
+    )(
+        features.reshape(rows, E),
+        partners.reshape(-1),
+        partners,
+        w_embed,
+        b_embed.reshape(1, D),
+        gain_query.reshape(1, D),
+        gain_memory.reshape(1, D),
+        w_query,
+        w_key,
+        w_value,
+        w_out,
+        gain_head.reshape(1, D),
+        w_head,
+        b_head,
+        points,
+        pair_pose,
+    )
+    return new_points, new_pose, loss.reshape(1)
 
 
 def layer_norm(values, gain):
@@ -174,7 +673,7 @@
 
 def solution(mesh):
     return jax.shard_map(
-        per_device,
+        fused if mesh.shape["img"] == NDEV else per_device,
         mesh=mesh,
         in_specs=(
             P(("groups", "img"), None, None),

time: 326 us -> 122 us (0.37)
  waiting for transfers between devices: 113 us -> 0 us
  Pallas kernels: 0 us -> 108 us
  matrix products: 59.9 us -> 0 us
  local copies, waits for them, and re-layouts: 48.9 us -> 10.5 us
  starting transfers between devices: 35.6 us -> 0 us
  other arithmetic: 31.1 us -> 0 us
  blocking collectives: 30.9 us -> 0 us
    all_to_all x2 -> x0, waiting for transfers between devices: 113 us -> none  [the longest x1 109 us: per_device(): lax.all_to_all(placed.astype(jnp.bfloat16).reshape(count, capacity, token...]
    pallas_call x0 -> x1, Pallas kernels: none -> 108 us  [fused(): pl.pallas_call(kernel, out_shape=(jax.ShapeDtypeStruct((IMGS, 3, TOK), F3...]
    dot_general x17 -> x0, matrix products: 59.9 us -> none  [the longest x1 15.6 us: per_device(): jnp.einsum('iphts,ipshd->ipthd', weights, value_views, preferred_element_...]
    all_to_all x2 -> x0, starting transfers between devices: 35.6 us -> none  [the longest x1 28.1 us: per_device(): lax.all_to_all(outgoing.astype(jnp.bfloat16), 'img', split_axis=0, concat...]
    psum x1 -> x0, blocking collectives: 30.9 us -> none  [per_device(): lax.psum((err_q + err_p, 2.0 * jnp.sum(certainty_level)), 'img')]
    reshape x8 -> x5, local copies, waits for them, and re-layouts: 32.8 us -> 5.81 us  [the longest x1 1.28 us: fused(): gain_query.reshape(1, D)]
    sub x1 -> x0, other arithmetic: 21.4 us -> none  [per_device(): expo = jnp.exp(scores - top)]
    gather x1 -> x0, local copies, waits for them, and re-layouts: 6.01 us -> none  [per_device(): jnp.take(arrived.reshape(slots, tokens_img, width), slot_of_view, axis=0)]
  transfers between devices with their start and end apart: 2 -> 0, of which waited for: 2 -> 0; matrix products, arithmetic and copies ran while one was open for 2% -> 0% of each run, Pallas kernels for 0% -> 0%
where the time goes in v1:
time: 122 us; the launch traced here: 121 us
  Pallas kernels  108 us (89%)
  local copies, waits for them, and re-layouts  10.5 us (9%)
  between operations  2.4 us (2%)
    pallas_call x1, Pallas kernels, fused(): pl.pallas_call(kernel, out_shape=(jax.ShapeDtypeStruct((IMGS, 3, TOK), F3...  108 us
    unnamed x6, local copies, waits for them, and re-layouts  4.72 us

profile of v1, /device:TPU:0, one launch (start us, length us, event | category | flops | bytes accessed | tf_op | source)
XLA Modules:
  0.0 121.4 jit_solution(13431394025367979057)
XLA Ops:
  0.6 1.3 %reshape.29.b_embed = f32[1,768]{1,0:T(1,128)} reshape(f32[768]{0:T(1024)} %param.18) | data formatting | bytes 6144 | tf_op jit(solution)/shard_map/reshape | solution.py:492
  1.9 1.3 %reshape.30.gain_query = f32[1,768]{1,0:T(1,128)} reshape(f32[768]{0:T(1024)} %param.19) | data formatting | bytes 6144 | tf_op jit(solution)/shard_map/reshape | solution.py:493
  3.2 1.2 %reshape.31.gain_memory = f32[1,768]{1,0:T(1,128)} reshape(f32[768]{0:T(1024)} %param.20) | data formatting | bytes 6144 | tf_op jit(solution)/shard_map/reshape | solution.py:494
  4.4 1.3 %reshape.32.gain_head = f32[1,768]{1,0:T(1,128)} reshape(f32[768]{0:T(1024)} %param.25) | data formatting | bytes 6144 | tf_op jit(solution)/shard_map/reshape | solution.py:499
  5.7 1.3 %copy.23.points = f32[8,3,64]{2,1,0:T(4,128)} copy(f32[8,3,64]{2,0,1:T(8,128)} %param.28) | data formatting | bytes 12288 | tf_op args[13]
  7.0 0.8 copy.21.partners_v
  7.8 0.0 copy-start
  7.8 0.7 reshape.28.partners_s
  8.5 0.0 copy-done
  8.5 108.5 %shard_map.166 = (f32[8,3,64]{2,1,0:T(4,128)}, f32[12,48]{1,0:T(8,128)}, f32[1,1]{1,0:T(1,128)}) custom-call(bf16[512,1024]{1,0:T(8,128)(2,1)} %bitcast.2, s32[768]{0:T(1024)} %reshape.28.partners_s, s32[128,6]{1,0:T(8,128)} %copy-done, bf16[1024,768]{1,0:T(8,128)(2,1)} %w_embed.1, f32[1,768]{1,0:T(1,128)} %reshape.29.b_embed, f32[1,768]{1,0:T(1,128)} %reshape.30.gain_query, ...), custom_call_target="tpu_custom_call" | custom-call | tf_op jit(solution)/shard_map/pallas_call | solution.py:432
  117.0 1.3 %copy.24 = f32[8,3,64]{2,0,1:T(8,128)} copy(f32[8,3,64]{2,1,0:T(4,128)} %get-tuple-element.12) | data formatting | bytes 12288
  118.3 1.3 %copy.27 = f32[12,48]{1,0:T(8,128)} copy(f32[12,48]{1,0:T(8,128)} %get-tuple-element.19) | data formatting | bytes 4608
Async XLA Ops:
  7.8 0.7 copy-start

commit v2 on v1

--- a/solution.py
+++ b/solution.py
@@ -36,8 +36,7 @@
 
 def kernel(
     features,
-    partners_s,
-    partners_v,
+    partners,
     w_embed,
     b_embed,
     gain_query,
@@ -133,14 +132,92 @@
         zero = (3 - j) // 3
         return zero * z + (1 - zero) * f
 
-    def forward_z(oz, piece):
-        @pl.when((oz < z) & (z < 3))
-        def _():
-            move(piece, UP).start()
-
-        @pl.when((oz > z) & (z > 0))
-        def _():
-            move(piece, DOWN).start()
+    def same(a, b):
+        return 1 // (1 + (a - b) * (a - b))
+
+    def ends(zz):
+        return (zz - 1) * (zz - 2) // 2
+
+    end = ends(z)
+
+    def pieces(tick, cc):
+        k, ch = (tick + 1) // 2, (tick - 1) % 2
+        two, three, five, seven = same(tick, 2), same(tick, 3), same(tick, 5), same(tick, 7)
+        yj = end * ((tick - 1) // 2) + (1 - end) * (tick // 2 - two)
+        ych = end * ((tick - 1) % 2) + (1 - end) * (two + five)
+        bz = origin_z(3 - 2 * three)
+        below = (rank_of(z - k, y, cc) * CHUNKS + ch, z - k >= 0)
+        above = (rank_of(z + k, y, cc) * CHUNKS + ch, z + k <= 3)
+        across = (rank_of(origin_z(yj), 1 - y, cc) * CHUNKS + ych, tick <= 6 + end)
+        turned = (
+            rank_of(bz, 1 - y, cc) * CHUNKS + 1,
+            (1 - end) * (three + five) + end * seven == 1,
+        )
+        turn = same(yj, 0) * ych * end
+        return below, above, across, turned, (k, ch, turn, bz)
+
+    def forward(tick, act, before=None):
+        below, above, across, turned, (k, ch, turn, bz) = pieces(tick, core)
+
+        @pl.when(below[1])
+        def _():
+            if before is not None:
+                before(below[0])
+
+            @pl.when(z < 3)
+            def _():
+                act(below[0], UP)
+
+            @pl.when(ch * ends(z - k) == 0)
+            def _():
+                act(below[0], ACROSS)
+
+            act(below[0], SIB)
+
+        @pl.when(above[1])
+        def _():
+            if before is not None:
+                before(above[0])
+
+            @pl.when(z > 0)
+            def _():
+                act(above[0], DOWN)
+
+            @pl.when(ch * ends(z + k) == 0)
+            def _():
+                act(above[0], ACROSS)
+
+            act(above[0], SIB)
+
+        @pl.when(across[1])
+        def _():
+            if before is not None:
+                before(across[0])
+
+            @pl.when((turn == 1) & (z == 0))
+            def _():
+                act(across[0], UP)
+
+            @pl.when((turn == 1) & (z == 3))
+            def _():
+                act(across[0], DOWN)
+
+            act(across[0], SIB)
+
+        @pl.when(turned[1])
+        def _():
+            if before is not None:
+                before(turned[0])
+
+            @pl.when((bz < z) & (z < 3))
+            def _():
+                act(turned[0], UP)
+
+            @pl.when((bz > z) & (z > 0))
+            def _():
+                act(turned[0], DOWN)
+
+            act(turned[0], SIB)
 
     def points_copy(peer, slot):
         return pltpu.make_async_remote_copy(
@@ -163,20 +240,20 @@
         ).wait_recv()
 
     all_points[own] = jnp.concatenate(
-        [points[:, 0, :], points[:, 1, :], points[:, 2, :], points[:, 2, :]], axis=1
+        [points[0], points[1], points[2], points[2]], axis=1
     )
 
     loads[0].wait()
     loads[1].wait()
     for ch in range(CHUNKS):
         rows = pl.ds(ch * CROWS, CROWS)
-        emb = (dot(feat[rows, :], we[...]) + b_embed[...]).astype(BF16)
+        emb = (dot(feat[rows, :], we[...]) + b_embed[...].reshape(1, D)).astype(BF16)
         embedded[rows, :] = emb
         emb_f = emb.astype(F32)
         center = emb_f - jnp.mean(emb_f, axis=-1, keepdims=True)
         unit = center * lax.rsqrt(jnp.mean(center * center, axis=-1, keepdims=True) + 1e-06)
-        memory[own * CHUNKS + ch] = (unit * gain_memory[...]).astype(BF16)
-        query_norm[rows, :] = (unit * gain_query[...]).astype(BF16)
+        memory[own * CHUNKS + ch] = (unit * gain_memory[...].reshape(1, D)).astype(BF16)
+        query_norm[rows, :] = (unit * gain_query[...].reshape(1, D)).astype(BF16)
         if ch == 0:
             pl.semaphore_wait(barrier, NDEV - 1)
             for k in range(1, NDEV):
@@ -220,48 +297,38 @@
         keys[at] = dot(rows, wk[...]).astype(BF16).reshape(CIMG, TOK, D)
         values[at] = dot(rows, wv[...]).astype(BF16).reshape(CIMG, TOK, D)
 
-    def exchange(step, carry):
-        j = 1 + step // CHUNKS
-        ch = step % CHUNKS
-        oz = origin_z(j)
-        oy = origin_z(j - 1)
-        from_z = rank_of(oz, y, core) * CHUNKS + ch
-        from_y = rank_of(oy, 1 - y, core) * CHUNKS + ch
-        arrive(from_z)
-        forward_z(oz, from_z)
-        move(from_z, ACROSS).start()
-        move(from_z, SIB).start()
-        project(from_z)
-        arrive(from_y)
-        move(from_y, SIB).start()
-        project(from_y)
-        sib_z = rank_of(oy, y, 1 - core) * CHUNKS + ch
-        arrive(sib_z)
-        project(sib_z)
+    def project_all(tick, cc, before=None):
+        for piece, valid in pieces(tick, cc)[:4]:
+
+            @pl.when(valid)
+            def _():
+                if before is not None:
+                    before(piece)
+                project(piece)
+
+    def own_sibling(ch, carry):
+        piece = rank_of(z, y, 1 - core) * CHUNKS + ch
+        arrive(piece)
+        project(piece)
         return carry
 
-    lax.fori_loop(0, 3 * CHUNKS, exchange, 0)
-
-    def finish(ch, carry):
-        oz = origin_z(3)
-        from_y = rank_of(oz, 1 - y, core) * CHUNKS + ch
-        arrive(from_y)
-        move(from_y, SIB).start()
-        sib_z = rank_of(oz, y, 1 - core) * CHUNKS + ch
-        arrive(sib_z)
-        project(sib_z)
-        project(from_y)
+    def exchange(tick, carry):
+        @pl.when(tick <= 7)
+        def _():
+            forward(tick, lambda piece, way: move(piece, way).start(), arrive)
+
+        @pl.when(tick >= 2)
+        def _():
+            project_all(tick - 1, 1 - core, arrive)
+
+        @pl.when(tick <= 7)
+        def _():
+            project_all(tick, core)
+
         return carry
 
-    def sibling_rest(step, carry):
-        sib_y = rank_of(origin_z(step // CHUNKS), 1 - y, 1 - core) * CHUNKS + step % CHUNKS
-        arrive(sib_y)
-        project(sib_y)
-        return carry
-
-    lax.fori_loop(0, 3 * CHUNKS, sibling_rest, 0)
-    lax.fori_loop(0, CHUNKS, finish, 0)
-    lax.fori_loop(3 * CHUNKS, 4 * CHUNKS, sibling_rest, 0)
+    lax.fori_loop(0, CHUNKS, own_sibling, 0)
+    lax.fori_loop(1, 9, exchange, 0)
 
     for k in range(1, NDEV):
         points_arrive((own + k) % NDEV, k)
@@ -270,7 +337,7 @@
     lane = lax.broadcasted_iota(jnp.int32, (TOK, 128), 1)
 
     def image(i, carry):
-        ids = [partners_s[own * VIEWS + i * PER + p] for p in range(PER)]
+        ids = [partners[p, own * IMGS + i] for p in range(PER)]
         key_rows = jnp.concatenate([keys[ids[p]] for p in range(PER)], axis=0)
         for g in range(3):
             scores = dot(
@@ -302,8 +369,10 @@
 
     x = [pred[:, c, :] + b_head[c] for c in range(7)]
     conf = 1.0 + jnp.exp(x[6])
-    mine = partners_v[pl.ds(pl.multiple_of(own * IMGS, IMGS), IMGS), :]
-    ids = jnp.concatenate([mine[:, p : p + 1] for p in range(PER)], axis=0)
+    view = lax.broadcasted_iota(jnp.int32, (VIEWS, 1), 0)
+    ids = jnp.zeros((VIEWS, 1), jnp.int32)
+    for v in range(VIEWS):
+        ids = jnp.where(view == v, partners[v // IMGS, own * IMGS + v % IMGS], ids)
     hot = (ids == lax.broadcasted_iota(jnp.int32, (VIEWS, ALL), 1)).astype(F32)
     row = lax.broadcasted_iota(jnp.int32, (VIEWS, VIEWS), 0)
     col = lax.broadcasted_iota(jnp.int32, (VIEWS, VIEWS), 1)
@@ -316,7 +385,7 @@
         off = pose[:, 9 + a : 10 + a]
         world_q = m[0] * x[0] + m[1] * x[1] + m[2] * x[2] + off
         world_p = m[0] * x[3] + m[1] * x[4] + m[2] * x[5] + off
-        chi = jnp.concatenate([points[:, a, :]] * PER, axis=0)
+        chi = jnp.concatenate([points[a]] * PER, axis=0)
         res_q.append(chi - world_q)
         res_p.append(partner_pts[:, a * TOK : (a + 1) * TOK] - world_p)
     cq = [conf * r for r in res_q]
@@ -367,26 +436,23 @@
     total_q = fold(conf)
     grad_q = [fold(c) for c in cq]
 
-    def drain(t, carry):
-        j = t // CHUNKS
-        ch = t % CHUNKS
-        oz = origin_z(j)
-        from_z = rank_of(oz, y, core) * CHUNKS + ch
-        move(from_z, ACROSS).wait_send()
-        move(from_z, SIB).wait_send()
-        move(rank_of(oz, 1 - y, core) * CHUNKS + ch, SIB).wait_send()
-
-        @pl.when((oz <= z) & (z < 3))
-        def _():
-            move(from_z, UP).wait_send()
-
-        @pl.when((oz >= z) & (z > 0))
-        def _():
-            move(from_z, DOWN).wait_send()
-
+    def drain(tick, carry):
+        forward(tick, lambda piece, way: move(piece, way).wait_send())
         return carry
 
-    lax.fori_loop(0, 4 * CHUNKS, drain, 0)
+    lax.fori_loop(1, 8, drain, 0)
+    for ch in range(CHUNKS):
+        piece = own * CHUNKS + ch
+        move(piece, ACROSS).wait_send()
+        move(piece, SIB).wait_send()
+
+        @pl.when(z < 3)
+        def _():
+            move(piece, UP).wait_send()
+
+        @pl.when(z > 0)
+        def _():
+            move(piece, DOWN).wait_send()
 
     for k in range(1, NDEV):
         peer = (own + k) % NDEV
@@ -403,7 +469,7 @@
     total = total_q + received[:, 192:256]
     for a in range(3):
         grad = grad_q[a] + received[:, a * TOK : (a + 1) * TOK]
-        new_points[:, a, :] = points[:, a, :] - 0.5 * grad / total
+        new_points[a] = points[a] - 0.5 * grad / total
     loss[...] = received[0:1, 256:257] / received[0:1, 320:321]
 
 
@@ -432,14 +498,13 @@
     new_points, new_pose, loss = pl.pallas_call(
         kernel,
         out_shape=(
-            jax.ShapeDtypeStruct((IMGS, 3, TOK), F32),
+            jax.ShapeDtypeStruct((3, IMGS, TOK), F32),
             jax.ShapeDtypeStruct((12, VIEWS), F32),
             jax.ShapeDtypeStruct((1, 1), F32),
         ),
         in_specs=[
             hbm,
             smem,
-            vmem,
             hbm,
             vmem,
             vmem,
@@ -486,23 +551,22 @@
         ),
     )(
         features.reshape(rows, E),
-        partners.reshape(-1),
-        partners,
+        partners.T,
         w_embed,
-        b_embed.reshape(1, D),
-        gain_query.reshape(1, D),
-        gain_memory.reshape(1, D),
+        b_embed,
+        gain_query,
+        gain_memory,
         w_query,
         w_key,
         w_value,
         w_out,
-        gain_head.reshape(1, D),
+        gain_head,
         w_head,
         b_head,
-        points,
+        points.transpose(1, 0, 2),
         pair_pose,
     )
-    return new_points, new_pose, loss.reshape(1)
+    return new_points.transpose(1, 0, 2), new_pose, loss.reshape(1)
 
 
 def layer_norm(values, gain):

time: 122 us -> 108 us (0.89)
  local copies, waits for them, and re-layouts: 10.5 us -> 2.6 us
  Pallas kernels: 108 us -> 103 us
    pallas_call x1, Pallas kernels: 108 us -> 103 us  [fused(): pl.pallas_call(kernel, out_shape=(jax.ShapeDtypeStruct((3, IMGS, TOK), F3...]
    reshape x5 -> x0, local copies, waits for them, and re-layouts: 5.81 us -> none  [the longest x1 1.28 us: fused(): gain_query.reshape(1, D)]
    unnamed x6 -> x2, local copies, waits for them, and re-layouts: 4.72 us -> 2.6 us
where the time goes in v2:
time: 108 us
  Pallas kernels  103 us (95%)
  local copies, waits for them, and re-layouts  2.6 us (2%)
  between operations  2.41 us (2%)
    pallas_call x1, Pallas kernels, fused(): pl.pallas_call(kernel, out_shape=(jax.ShapeDtypeStruct((3, IMGS, TOK), F3...  103 us
    unnamed x2, local copies, waits for them, and re-layouts  2.6 us

profile of v2, /device:TPU:0, one launch (start us, length us, event | category | flops | bytes accessed | tf_op | source)
XLA Modules:
  0.0 107.6 jit_solution(4926108275523956846)
XLA Ops:
  0.6 102.6 %shard_map.166 = (f32[3,8,64]{2,1,0:T(8,128)}, f32[12,48]{1,0:T(8,128)}, f32[1,1]{1,0:T(1,128)}) custom-call(bf16[512,1024]{1,0:T(8,128)(2,1)} %bitcast.5, s32[6,128]{1,0:T(8,128)} %bitcast.8, bf16[1024,768]{1,0:T(8,128)(2,1)} %w_embed.1, f32[768]{0:T(1024)} %b_embed.1, f32[768]{0:T(1024)} %gain_query.1, f32[768]{0:T(1024)} %gain_memory.1, ...), custom_call_target="tpu_custom_call" | custom-call | tf_op jit(solution)/shard_map/pallas_call | solution.py:498
  103.2 1.3 %copy.21 = f32[8,3,64]{2,0,1:T(8,128)} copy(f32[8,3,64]{2,0,1:T(8,128)} %bitcast.7) | data formatting | bytes 12288
  104.5 1.3 %copy.22 = f32[12,48]{1,0:T(8,128)} copy(f32[12,48]{1,0:T(8,128)} %get-tuple-element.13) | data formatting | bytes 4608

commit v3 on v2

--- a/solution.py
+++ b/solution.py
@@ -256,21 +256,22 @@
         query_norm[rows, :] = (unit * gain_query[...].reshape(1, D)).astype(BF16)
         if ch == 0:
             pl.semaphore_wait(barrier, NDEV - 1)
+        piece = own * CHUNKS + ch
+
+        move(piece, ACROSS).start()
+
+        @pl.when(z < 3)
+        def _():
+            move(piece, UP).start()
+
+        @pl.when(z > 0)
+        def _():
+            move(piece, DOWN).start()
+
+        move(piece, SIB).start()
+        if ch == 0:
             for k in range(1, NDEV):
                 points_copy((own + k) % NDEV, k).start()
-        piece = own * CHUNKS + ch
-
-        move(piece, ACROSS).start()
-
-        @pl.when(z < 3)
-        def _():
-            move(piece, UP).start()
-
-        @pl.when(z > 0)
-        def _():
-            move(piece, DOWN).start()
-
-        move(piece, SIB).start()
 
     loads[2].wait()
     group = lax.broadcasted_iota(jnp.int32, (256, 256), 0) // 64
@@ -327,12 +328,23 @@
 
         return carry
 
-    lax.fori_loop(0, CHUNKS, own_sibling, 0)
-    lax.fori_loop(1, 9, exchange, 0)
-
     for k in range(1, NDEV):
         points_arrive((own + k) % NDEV, k)
         points_copy((own + k) % NDEV, k).wait_send()
+
+    view = lax.broadcasted_iota(jnp.int32, (VIEWS, 1), 0)
+    ids = jnp.zeros((VIEWS, 1), jnp.int32)
+    for v in range(VIEWS):
+        ids = jnp.where(view == v, partners[v // IMGS, own * IMGS + v % IMGS], ids)
+    hot = (ids == lax.broadcasted_iota(jnp.int32, (VIEWS, ALL), 1)).astype(F32)
+    row = lax.broadcasted_iota(jnp.int32, (VIEWS, VIEWS), 0)
+    col = lax.broadcasted_iota(jnp.int32, (VIEWS, VIEWS), 1)
+    perm = ((row % IMGS) * PER + row // IMGS == col).astype(F32)
+    pose = dot(perm, pair_pose[...], ((1,), (1,)), HI)
+    partner_pts = dot(hot, all_points[...].reshape(ALL, 256), precision=HI)
+
+    lax.fori_loop(0, CHUNKS, own_sibling, 0)
+    lax.fori_loop(1, 9, exchange, 0)
 
     lane = lax.broadcasted_iota(jnp.int32, (TOK, 128), 1)
 
@@ -369,16 +381,6 @@
 
     x = [pred[:, c, :] + b_head[c] for c in range(7)]
     conf = 1.0 + jnp.exp(x[6])
-    view = lax.broadcasted_iota(jnp.int32, (VIEWS, 1), 0)
-    ids = jnp.zeros((VIEWS, 1), jnp.int32)
-    for v in range(VIEWS):
-        ids = jnp.where(view == v, partners[v // IMGS, own * IMGS + v % IMGS], ids)
-    hot = (ids == lax.broadcasted_iota(jnp.int32, (VIEWS, ALL), 1)).astype(F32)
-    row = lax.broadcasted_iota(jnp.int32, (VIEWS, VIEWS), 0)
-    col = lax.broadcasted_iota(jnp.int32, (VIEWS, VIEWS), 1)
-    perm = ((row % IMGS) * PER + row // IMGS == col).astype(F32)
-    pose = dot(perm, pair_pose[...], ((1,), (1,)), HI)
-    partner_pts = dot(hot, all_points[...].reshape(ALL, 256), precision=HI)
     res_q, res_p = [], []
     for a in range(3):
         m = [pose[:, 3 * a + b : 3 * a + b + 1] for b in range(3)]

time: 108 us -> 108 us (level)
  no operation moved by 1% of the time
where the time goes in v3:
time: 108 us; the launch traced here: 107 us
  Pallas kernels  102 us (94%)
  local copies, waits for them, and re-layouts  2.6 us (2%)
  between operations  2.41 us (2%)
    pallas_call x1, Pallas kernels, fused(): pl.pallas_call(kernel, out_shape=(jax.ShapeDtypeStruct((3, IMGS, TOK), F3...  102 us
    unnamed x2, local copies, waits for them, and re-layouts  2.6 us

profile of v3, /device:TPU:0, one launch (start us, length us, event | category | flops | bytes accessed | tf_op | source)
XLA Modules:
  0.0 107.3 jit_solution(7457404382902796221)
XLA Ops:
  0.6 102.3 %shard_map.166 = (f32[3,8,64]{2,1,0:T(8,128)}, f32[12,48]{1,0:T(8,128)}, f32[1,1]{1,0:T(1,128)}) custom-call(bf16[512,1024]{1,0:T(8,128)(2,1)} %bitcast.5, s32[6,128]{1,0:T(8,128)} %bitcast.8, bf16[1024,768]{1,0:T(8,128)(2,1)} %w_embed.1, f32[768]{0:T(1024)} %b_embed.1, f32[768]{0:T(1024)} %gain_query.1, f32[768]{0:T(1024)} %gain_memory.1, ...), custom_call_target="tpu_custom_call" | custom-call | tf_op jit(solution)/shard_map/pallas_call | solution.py:500
  102.9 1.3 %copy.21 = f32[8,3,64]{2,0,1:T(8,128)} copy(f32[8,3,64]{2,0,1:T(8,128)} %bitcast.7) | data formatting | bytes 12288
  104.2 1.3 %copy.22 = f32[12,48]{1,0:T(8,128)} copy(f32[12,48]{1,0:T(8,128)} %get-tuple-element.13) | data formatting | bytes 4608
